TPU v7x, 256 devices: a whole 4x4x8 slice. The times are simulated.
256 devices in a mesh: role: 2 (over z_lo), seq: 16 (over z_hi, y), tensor: 8 (over x, core).
Axes of the slice: x: 4, y: 4, z: 8 (z_hi: 4, z_lo: 2; z = z_hi * 2 + z_lo), core: 2. Of those that a mesh axis runs over, the one named last changes fastest.
Arguments:
- queries: bfloat16 [2, 2048, 8192], P('role', 'seq', 'tensor'), may hold values from -6 to 6
- new_kv: bfloat16 [2, 2048, 8, 256], P('role', 'seq', 'tensor'), may hold values from -12 to 12
- prefix_kv: bfloat16 [16384, 8, 256], P('seq', 'tensor'), may hold values from -12 to 12
- cache_kv: bfloat16 [512, 512, 8, 256], P('seq', None, 'tensor'), may hold values from -12 to 12
- prompt_lengths: int32 [8], replicated, may hold values from 1 to 1536, 2048 in all
- cache_lengths: int32 [512], replicated, may hold values from 2 to 512, as said below
- prompt_slots: int32 [8], replicated, may hold values from 0 to 511, as said below
Outputs:
- attended: bfloat16 [2, 2048, 8192], P('role', 'seq', 'tensor')
Inputs may be any that keep to these rules, and one draw needn't show every extreme that they name: `prompt_lengths`: the lengths sum to 2048; one is 1536. `cache_lengths`: some row uses all 512 positions. `prompt_slots`: no row takes two prompts; row 0 and row 511 each take one.
All inputs are finite; a program needn't handle non-finite values.
Results may differ from a plain program's by a relative error of at most 0.0045.
Values may be sent and summed in bfloat16 or wider, within the bound.
A program may use at most 192 MiB of HBM per device.

v0:
```python
import jax
import jax.numpy as jnp
from jax import lax
from jax.sharding import PartitionSpec as P

LOWEST = -1e30


def from_behind(value, axis, steps):
    count = lax.axis_size(axis)
    first, last = (max(0, -steps), min(count, count - steps))
    return lax.ppermute(value, axis, [(source, source + steps) for source in range(first, last)])


def segment_of(prompt_lengths, count):
    ends = jnp.cumsum(prompt_lengths)
    places = jnp.arange(count, dtype=jnp.int32)
    return jnp.sum((places[:, None] >= ends[None, :]).astype(jnp.int32), axis=1)


def prompt_of_row(prompt_slots, count):
    row_ids = jnp.arange(count, dtype=jnp.int32)
    labels = jnp.arange(1, prompt_slots.shape[0] + 1, dtype=jnp.int32)
    hits = jnp.where(prompt_slots[None, :] == row_ids[:, None], labels[None, :], 0)
    return jnp.sum(hits, axis=1) - 1


def empty_state(leading, head_size):
    return (
        jnp.full(leading, LOWEST, jnp.float32),
        jnp.zeros(leading, jnp.float32),
        jnp.zeros(leading + (head_size,), jnp.float32),
    )


def absorb(state, query_vector, index_pairs, visible_mask):
    highest, total, weighted = state
    head_size = query_vector.shape[-1]
    key_vectors = index_pairs[..., :head_size]
    value_vectors = index_pairs[..., head_size:]
    if index_pairs.ndim == 3:
        scores = jnp.einsum(
            "rhqd,nhd->rhqn", query_vector, key_vectors, preferred_element_type=jnp.float32
        )
    else:
        scores = jnp.einsum(
            "rhqd,rnhd->rhqn", query_vector, key_vectors, preferred_element_type=jnp.float32
        )
    scores = scores * head_size ** (-0.5)
    if visible_mask is not None:
        scores = jnp.where(visible_mask, scores, LOWEST)
    raised = jnp.maximum(highest, jnp.max(scores, axis=3))
    weights = jnp.exp(scores - raised[..., None])
    if visible_mask is not None:
        weights = jnp.where(visible_mask, weights, 0.0)
    shrink = jnp.exp(highest - raised)
    total = total * shrink + jnp.sum(weights, axis=3)
    rounded = weights.astype(jnp.bfloat16)
    if index_pairs.ndim == 3:
        mixed = jnp.einsum(
            "rhqn,nhd->rhqd", rounded, value_vectors, preferred_element_type=jnp.float32
        )
    else:
        mixed = jnp.einsum(
            "rhqn,rnhd->rhqd", rounded, value_vectors, preferred_element_type=jnp.float32
        )
    return (raised, total, weighted * shrink[..., None] + mixed)


def prefill_side(queries, new_kv, prefix_kv, segment, on_prefill):
    tokens = queries.shape[1]
    kv_heads = new_kv.shape[2]
    head_size = new_kv.shape[3] // 2
    group = queries.shape[2] // (kv_heads * head_size)
    query_vector = queries[0].reshape(tokens, kv_heads, group, head_size)
    query_vector = jnp.transpose(query_vector, (1, 0, 2, 3)).reshape(
        1, kv_heads, tokens * group, head_size
    )
    state = empty_state((1, kv_heads, tokens * group), head_size)
    piece = lax.all_gather(prefix_kv, "seq", axis=0, tiled=True)
    state = lax.cond(
        on_prefill, lambda kept: absorb(kept, query_vector, piece, None), lambda kept: kept, state
    )
    first_piece = lax.axis_index("seq") * tokens
    mine = lax.dynamic_slice_in_dim(segment, first_piece, tokens)
    own_places = first_piece + jnp.arange(tokens, dtype=jnp.int32)

    def add_stretch(carry, piece):
        count = piece.shape[0]
        places = jnp.arange(count, dtype=jnp.int32)
        inner = (places[None, :] <= own_places[:, None]) & (segment[None, :] == mine[:, None])
        visible_mask = jnp.repeat(inner, group, axis=0)[None, None]
        return absorb(carry, query_vector, piece, visible_mask)

    add_piece = lax.all_gather(new_kv[0], "seq", axis=0, tiled=True)
    state = lax.cond(
        on_prefill, lambda kept: add_stretch(kept, add_piece), lambda kept: kept, state
    )
    highest, total, weighted = state
    safe_total = jnp.where(total > 0.0, total, 1.0)
    attention_output = (weighted / safe_total[..., None]).reshape(
        kv_heads, tokens, group, head_size
    )
    attention_output = jnp.transpose(attention_output, (1, 0, 2, 3)).reshape(
        1, tokens, kv_heads * group * head_size
    )
    return attention_output.astype(jnp.bfloat16)


def decode_side(
    queries, new_kv, every_position, cache_kv, cache_lengths, prompt_row, segment, first_row
):
    tokens = queries.shape[1]
    kv_heads = new_kv.shape[2]
    head_size = new_kv.shape[3] // 2
    group = queries.shape[2] // (kv_heads * head_size)
    own_rows = cache_kv.shape[0]
    span = cache_kv.shape[1]
    steps = tokens // own_rows
    query_rows = steps * group
    shaped = queries[0].reshape(own_rows, steps, kv_heads, group, head_size)
    query_vector = jnp.transpose(shaped, (0, 2, 1, 3, 4)).reshape(
        own_rows, kv_heads, query_rows, head_size
    )
    fresh = new_kv[0].reshape(own_rows, steps, kv_heads, 2 * head_size)
    step_of_row = jnp.arange(query_rows, dtype=jnp.int32) // group
    step_visible = (jnp.arange(steps, dtype=jnp.int32)[None, :] <= step_of_row[:, None])[None, None]
    lengths = lax.dynamic_slice_in_dim(cache_lengths, first_row, own_rows)
    prompts = lax.dynamic_slice_in_dim(prompt_row, first_row, own_rows)
    live = (jnp.arange(span, dtype=jnp.int32)[None, :] < lengths[:, None])[:, None, None, :]
    matched = (segment[None, :] == prompts[:, None])[:, None, None, :]
    state = absorb(
        empty_state((own_rows, kv_heads, query_rows), head_size), query_vector, cache_kv, live
    )
    state = absorb(state, query_vector, every_position, matched)
    state = absorb(state, query_vector, fresh, step_visible)
    attention_output = (state[2] / state[1][..., None]).reshape(
        own_rows, kv_heads, steps, group, head_size
    )
    attention_output = jnp.transpose(attention_output, (0, 2, 1, 3, 4))
    return attention_output.reshape(1, tokens, kv_heads * group * head_size).astype(jnp.bfloat16)


def body(queries, new_kv, prefix_kv, cache_kv, prompt_lengths, cache_lengths, prompt_slots):
    segment = segment_of(prompt_lengths, new_kv.shape[1] * lax.axis_size("seq"))
    prompt_row = prompt_of_row(prompt_slots, cache_kv.shape[0] * lax.axis_size("seq"))
    on_prefill = lax.axis_index("role") == 0
    first_row = lax.axis_index("seq") * cache_kv.shape[0]
    handed = from_behind(new_kv, "role", 1)
    every_position = lax.all_gather(handed[0], "seq", axis=0, tiled=True)
    prefill_output = prefill_side(queries, new_kv, prefix_kv, segment, on_prefill)
    attention_output = lax.cond(
        on_prefill,
        lambda: prefill_output,
        lambda: decode_side(
            queries, new_kv, every_position, cache_kv, cache_lengths, prompt_row, segment, first_row
        ),
    )
    return attention_output


def solution(mesh):
    return jax.shard_map(
        body,
        mesh=mesh,
        in_specs=(
            P("role", "seq", "tensor"),
            P("role", "seq", "tensor", None),
            P("seq", "tensor", None),
            P("seq", None, "tensor", None),
            P(),
            P(),
            P(),
        ),
        out_specs=P("role", "seq", "tensor"),
        check_vma=False,
    )
```

profile of v0, /device:TPU:65, one launch (start us, length us, event | category | flops | bytes accessed | tf_op | source)
XLA Modules:
  0.0 282.3 jit_solution(18214437058207086738)
XLA Ops:
  6.5 0.0 all-gather.8.cloned.1.call-start
  6.5 3.5 %collective-permute-start = (bf16[1,128,1,256]{3,1,2,0:T(8,128)(2,1)}, bf16[1,128,1,256]{3,1,2,0:T(8,128)(2,1)S(1)}, u32[]{:S(2)}, u32[]{:S(2)}) collective-permute-start(bf16[1,128,1,256]{3,1,2,0:T(8,128)(2,1)} %param.14), channel_id=1, source_target_pairs={{0,128},{1,129},{2,130},{3,131},{4,132},{5,133},{6,134},{7,135},{8... | collective-permute-start | bytes 196616 | tf_op jit(solution)/shard_map/ppermute | solution.py:12
  10.1 1.6 collective-permute-done
  11.7 0.0 copy-start.8
  11.7 0.6 copy-done.8
  12.3 0.0 all-gather.8.cloned.1.call-update
  12.4 0.0 all-gather.6.cloned.1.call-start
  12.4 0.7 all-gather.6.cloned.1.call-update
  13.1 0.0 all-gather.10.cloned.1.call-start
  13.2 0.7 all-gather.10.cloned.1.call-update
  13.9 1.1 reshape_transpose_reshape_squeeze.3
  14.9 0.8 reduce-window.8
  15.8 0.1 convert_reduce_fusion
  15.9 49.9 %all-gather.8.cloned.1.call-done = bf16[1,2048,1,256]{3,1,2,0:T(8,128)(2,1)} async-done(((bf16[1,128,1,256]{3,1,2,0:T(8,128)(2,1)}), bf16[1,2048,1,256]{3,1,2,0:T(8,128)(2,1)}) %all-gather.8.cloned.1.call-update) | async-done | bytes 1048592 | tf_op jit(solution)/shard_map/all_gather | solution.py:150
  65.8 119.5 %all-gather.6.cloned.1.call-done = bf16[16384,1,256]{2,0,1:T(8,128)(2,1)} async-done(((bf16[1024,1,256]{2,0,1:T(8,128)(2,1)}), bf16[16384,1,256]{2,0,1:T(8,128)(2,1)}) %all-gather.6.cloned.1.call-update) | async-done | bytes 8388624 | tf_op jit(solution)/shard_map/all_gather | solution.py:80
  185.2 74.2 %conditional.8 = (f32[1,1,1024]{2,1,0:T(1,128)}, f32[1,1,1024]{2,1,0:T(1,128)S(1)}, f32[1,1,1024,128]{3,2,0,1:T(8,128)S(1)}) conditional(s32[]{:T(128)} %convert_element_type.55, () %tuple.48, (bf16[16384,1,256]{2,0,1:T(8,128)(2,1)}, bf16[1,1,1024,128]{3,2,1,0:T(8,128)(2,1)S(1)}) %tuple.49), branch_computations={%region_3.4_spmd, %region_4.7_spmd} | conditional | flops 8724287488 | bytes 210546720 | solution.py:81
  185.2 25.9 %multiply_reduce_fusion = (f32[1024]{0:T(1024)S(1)}, f32[16384,1024]{1,0:T(8,128)}) fusion(bf16[1,1,1024,128]{3,2,1,0:T(8,128)(2,1)S(1)} %get-tuple-element.136, bf16[16384,1,256]{2,0,1:T(8,128)(2,1)} %get-tuple-element.135), kind=kOutput, calls=%fused_computation.2 | convolution fusion | flops 4328520704 | bytes 71569408 | tf_op jit(solution)/shard_map/cond/branch_1_fun/rhqd,nhd->rhqn/dot_general | solution.py:42
  211.2 0.6 exponential_multiply_fusion
  211.8 22.0 %fusion.2 = f32[1024]{0:T(1024)S(1)} fusion(f32[16384,1024]{1,0:T(8,128)} %get-tuple-element.261, f32[1024]{0:T(1024)} %get-tuple-element.259), kind=kLoop, calls=%fused_computation.4 | loop fusion | flops 50330624 | bytes 67117056 | tf_op jit(solution)/shard_map/cond/branch_1_fun/reduce_sum | solution.py:57
  233.8 0.7 multiply_add_fusion
  234.5 25.0 %fusion.21 = f32[1,1,1024,128]{3,2,0,1:T(8,128)S(1)} fusion(bf16[16384,1,256]{2,0,1:T(8,128)(2,1)} %get-tuple-element.135, f32[16384,1024]{1,0:T(8,128)} %get-tuple-element.261, f32[1024]{0:T(1024)} %get-tuple-element.259, f32[1024]{0:T(1024)S(1)} %get-tuple-element.258), kind=kOutput, calls=%fused_computation.14 | convolution fusion | flops 4345430016 | bytes 71835648 | tf_op jit(solution)/shard_map/cond/branch_1_fun/rhqn,nhd->rhqd/dot_general | solution.py:60
  259.5 0.0 all-gather.10.cloned.1.call-done
  259.5 0.0 copy-start.1
  259.5 0.0 copy-start.3
  259.5 0.0 copy-start.5
  259.6 0.0 copy-start.11
  259.6 14.9 %conditional.9 = ((f32[1,1,1024]{2,1,0:T(1,128)S(1)}, f32[1,1,1024,128]{3,2,0,1:T(8,128)S(1)})) conditional(s32[]{:T(128)} %convert_element_type.55, (f32[1,1,1024]{2,1,0:T(1,128)S(1)}, f32[1,1,1024,128]{3,2,0,1:T(8,128)S(1)}) %tuple.50, (s32[]{:T(128)}, s32[128]{0:T(128)S(1)}, s32[2048]{0:T(1024)S(1)}, bf16[2048,1,256]{2,0,1:T(8,128)(2,1)}, ...), branch_computations={%region_7.8_spmd, %region_8.11_spmd} | conditional | flops 1102055552 | bytes 44895336 | solution.py:96
  259.8 0.1 dynamic_slice.9
  259.8 0.3 fusion.40
  260.2 1.0 broadcast_bitcast_fusion
  261.2 4.0 %copy.21 = pred[1,1,1024,2048]{2,3,0,1:T(32,128)(4,1)S(1)} copy(pred[1,1,1024,2048]{3,2,1,0:T(32,128)(4,1)S(1)} %broadcast_bitcast_fusion) | data formatting | bytes 4194304 | tf_op jit(solution)/shard_map/cond/branch_1_fun/broadcast_in_dim;cond/branch_1_fun/reshape | solution.py:92
  265.1 2.6 fusion.28
  267.8 0.0 copy-start.2
  267.8 0.8 max.44
  268.6 2.5 fusion.30
  271.0 0.7 multiply_add_fusion.1
  271.8 0.0 copy-done.2
  271.8 2.7 fusion.37
  274.5 0.0 copy-done.1
  274.5 0.0 copy-done.3
  274.5 0.0 copy-done.5
  274.5 0.0 copy-done.11
  274.5 0.6 conditional.10
  274.8 0.2 bitcast_divide_fusion
  275.0 0.1 reshape_transpose_reshape.2
  275.1 0.0 copy-start.4
  275.1 0.7 copy-done.4
  (5 shorter events, 0.0 us)
Async XLA Ops:
  6.5 59.2 %all-gather.8.cloned.1.call-start = ((), (), s32[]{:S(2)}) async-start(), calls=%async_computation.1 | async-start | bytes 1114112 | tf_op jit(solution)/shard_map/all_gather | solution.py:150
  6.5 5.2 %collective-permute-start = (bf16[1,128,1,256]{3,1,2,0:T(8,128)(2,1)}, bf16[1,128,1,256]{3,1,2,0:T(8,128)(2,1)S(1)}, u32[]{:S(2)}, u32[]{:S(2)}) collective-permute-start(bf16[1,128,1,256]{3,1,2,0:T(8,128)(2,1)} %param.14), channel_id=1, source_target_pairs={{0,128},{1,129},{2,130},{3,131},{4,132},{5,133},{6,134},{7,135},{8... | collective-permute-start | bytes 196616 | tf_op jit(solution)/shard_map/ppermute | solution.py:12
  11.7 0.6 copy-start.8
  12.4 172.9 %all-gather.6.cloned.1.call-start = ((), (), s32[]{:S(2)}) async-start(), calls=%async_computation | async-start | bytes 8912896 | tf_op jit(solution)/shard_map/all_gather | solution.py:80
  13.1 246.4 %all-gather.10.cloned.1.call-start = ((), (), s32[]{:S(2)}) async-start(), calls=%async_computation.2 | async-start | bytes 1114112 | tf_op jit(solution)/shard_map/all_gather | solution.py:95
  259.5 14.9 %copy-start.1 = (bf16[1,128,1024]{2,1,0:T(8,128)(2,1)S(1)}, bf16[1,128,1024]{2,1,0:T(8,128)(2,1)}, u32[]{:S(2)}) copy-start(bf16[1,128,1024]{2,1,0:T(8,128)(2,1)} %param.13) | copy-start | bytes 786436
  259.5 14.9 %copy-start.3 = (bf16[1,2048,1,256]{3,1,2,0:T(8,128)(2,1)S(1)}, bf16[1,2048,1,256]{3,1,2,0:T(8,128)(2,1)}, u32[]{:S(2)}) copy-start(bf16[1,2048,1,256]{3,1,2,0:T(8,128)(2,1)} %all-gather.8.cloned.1.call-done) | copy-start | bytes 3145732
  259.5 14.9 %copy-start.5 = (bf16[1,128,1,256]{3,1,2,0:T(8,128)(2,1)S(1)}, bf16[1,128,1,256]{3,1,2,0:T(8,128)(2,1)}, u32[]{:S(2)}) copy-start(bf16[1,128,1,256]{3,1,2,0:T(8,128)(2,1)} %param.14) | copy-start | bytes 196612
  259.6 14.9 %copy-start.11 = (s32[8]{0:T(128)S(1)}, s32[8]{0:T(128)}, u32[]{:S(2)}) copy-start(s32[8]{0:T(128)} %param.19) | copy-start | bytes 100
  267.8 4.0 %copy-start.2 = (bf16[2048,1,256]{2,0,1:T(8,128)(2,1)S(1)}, bf16[2048,1,256]{2,0,1:T(8,128)(2,1)}, u32[]{:S(2)}) copy-start(bf16[2048,1,256]{2,0,1:T(8,128)(2,1)} %get-tuple-element.142) | copy-start | bytes 3145732 | tf_op jit(solution)/shard_map/cond
  275.1 0.7 copy-start.4
Sparse Core Ops, SparseCore 0:
  12.5 53.2 all-gather.7
  68.2 117.0 all-gather.5
  187.7 48.6 all-gather.9
where the time goes:
time: 283 us; the launch traced here: 282 us
  waiting for transfers between devices  172 us (61%)
  matrix products  56.3 us (20%)
  other arithmetic  28.7 us (10%)
  between operations  13.2 us (5%)
  local copies, waits for them, and re-layouts  7.58 us (3%)
  starting transfers between devices  3.62 us (1%)
    all_gather x1, waiting for transfers between devices, prefill_side(): piece = lax.all_gather(prefix_kv, 'seq', axis=0, tiled=True)  119 us
    all_gather x1, waiting for transfers between devices, body(): every_position = lax.all_gather(handed[0], 'seq', axis=0, tiled=True)  49.9 us
    dot_general x2, matrix products, absorb(): jnp.einsum('rhqd,nhd->rhqn', query_vector, key_vectors, preferred_element...  28.6 us
    dot_general x2, matrix products, absorb(): jnp.einsum('rhqn,nhd->rhqd', rounded, value_vectors, preferred_element_ty...  27.7 us
    reduce_sum x2, other arithmetic, absorb(): total = total * shrink + jnp.sum(weights, axis=3)  24.4 us
  transfers between devices with their start and end apart: 4, of which 3 were waited for; matrix products, arithmetic and copies ran while one was open for 27% of the time, Pallas kernels for 0%

commit v1 on v0

v1 whole, which is shorter than its diff:
```python
import functools
import math

import jax
import jax.numpy as jnp
from jax import lax
from jax.experimental import pallas as pl
from jax.experimental.pallas import tpu as pltpu
from jax.sharding import PartitionSpec as P

MESH = pl.DeviceIdType.MESH
NEG = -1e30
D = 128
SCALE = math.log2(math.e) / math.sqrt(D)
RB = 256
NT = (((1,), (1,)), ((), ()))
NN = (((1,), (0,)), ((), ()))
F32 = jnp.float32
BF16 = jnp.bfloat16


def dot(a, b, dims):
    return lax.dot_general(a, b, dims, preferred_element_type=F32)


def with_ones(v):
    return jnp.concatenate([v, jnp.ones_like(v)], axis=1)


def column(row):
    return jnp.transpose(jnp.broadcast_to(row, (D, D)))


def kernel(
    lengths_ref, cache_len_ref, slots_ref, q_ref, new_ref, prefix_ref, cache_ref,
    out_ref,
    kvb, qall, strall, acc, m, l, ob, ls, ro, rl, cacheb, sa, sb, ma, mb,
    pq, pacc, pm, psum,
    local_sem, cache_sem, kv_send, kv_recv, q_send, q_recv, str_send, str_recv,
    slab_send, slab_recv, o_send, o_recv, l_send, l_recv,
):
    role = lax.axis_index("role")
    seq = lax.axis_index("seq")
    tensor = lax.axis_index("tensor")
    zh, y = seq // 4, lax.rem(seq, 4)
    z = zh * 2 + role

    def dev(dy, dz):
        yy = lax.rem(y + dy + 8, 4)
        zz = lax.rem(z + dz + 8, 8)
        return (lax.rem(zz, 2), (zz // 2) * 4 + yy, tensor)

    def remote(src, dst, ss, rs, dy, dz):
        return pltpu.make_async_remote_copy(
            src_ref=src, dst_ref=dst, send_sem=ss, recv_sem=rs,
            device_id=dev(dy, dz), device_id_type=MESH,
        )

    is_pre = role == 0
    is_dec = role == 1
    half = 512

    own_kv = pltpu.make_async_copy(prefix_ref, kvb.at[0], local_sem.at[0])
    own_kv.start()
    own_q = pltpu.make_async_copy(q_ref, qall.at[pl.ds(0, 1024)], local_sem.at[1])
    own_q.start()

    def cache_copy(g):
        rows = pl.ds(g * 4, 4)
        return pltpu.make_async_copy(cache_ref.at[rows], cacheb.at[rows], cache_sem.at[g])

    @pl.when(is_dec)
    def _():
        for g in range(8):
            cache_copy(g).start()

    barrier = pltpu.get_barrier_semaphore()
    peers = [(0, dz) for dz in range(1, 8)] + [(1, 0), (2, 0), (3, 0)]
    for dy, dz in peers:
        pl.semaphore_signal(barrier, inc=1, device_id=dev(dy, dz), device_id_type=MESH)
    pl.semaphore_wait(barrier, len(peers))

    slot = strall.at[zh, y]
    stretch_y = [remote(slot, slot, str_send.at[i], str_recv.at[i], dy, 0) for i, dy in enumerate((1, 3, 2))]
    stretch_z = remote(slot, slot, str_send.at[3], str_recv.at[3], 0, 1)
    first, second = pl.ds(0, half), pl.ds(half, half)
    kv_copies = [
        remote(kvb.at[0, first], kvb.at[1, first], kv_send.at[0], kv_recv.at[0], 1, 0),
        remote(kvb.at[0, second], kvb.at[1, second], kv_send.at[1], kv_recv.at[1], 3, 0),
        remote(kvb.at[0, second], kvb.at[2, first], kv_send.at[2], kv_recv.at[2], 1, 0),
        remote(kvb.at[0, first], kvb.at[2, second], kv_send.at[3], kv_recv.at[3], 3, 0),
        remote(kvb.at[1, first], kvb.at[3, first], kv_send.at[4], kv_recv.at[4], 1, 0),
        remote(kvb.at[1, second], kvb.at[3, second], kv_send.at[5], kv_recv.at[5], 3, 0),
    ]
    far_q = qall.at[pl.ds(1024, 1024)]
    far_half = qall.at[pl.ds(2048, half)]
    q_copies = [
        remote(qall.at[pl.ds(0, 1024)], far_q, q_send.at[0], q_recv.at[0], 0, -1),
        remote(qall.at[pl.ds(0, 1024)], far_q, q_send.at[1], q_recv.at[0], 0, 2),
        remote(qall.at[pl.ds(0, half)], far_half, q_send.at[2], q_recv.at[1], 0, -3),
        remote(qall.at[pl.ds(half, half)], far_half, q_send.at[3], q_recv.at[1], 0, 4),
    ]
    slab = strall.at[zh]
    slab_copies = [
        remote(slab, slab, slab_send.at[i], slab_recv.at[i], 0, dz) for i, dz in enumerate((2, -2, 4))
    ]

    @pl.when(is_pre)
    def _():
        strall[zh, y] = new_ref[...]
        stretch_z.start()
        for c in stretch_y:
            c.start()

    own_kv.wait()
    for c in kv_copies[:4]:
        c.start()
    own_q.wait()

    @pl.when(is_pre)
    def _():
        for c in q_copies:
            c.start()

    def clear(b, _):
        rows = pl.ds(pl.multiple_of(b * D, D), D)
        acc[rows, :] = jnp.zeros((D, D), F32)
        l[rows, :] = jnp.zeros((D, D), F32)
        m[rows, :] = jnp.full((D, D), NEG, F32)
        return 0

    lax.fori_loop(0, 20, clear, 0)

    def block(row0, i):
        return pl.ds(pl.multiple_of(row0 + i * RB, RB), RB)

    def scores(rows, kvi, s, mx):
        x = dot(qall[rows, :], kvb[kvi, :, :D], NT)
        s[...] = x
        mx[...] = jnp.broadcast_to(jnp.max(x, axis=1, keepdims=True) * SCALE, mx.shape)

    def absorb(rows, kvi, s, mx):
        old = m[rows, :]
        new = jnp.maximum(old, mx[...])
        shrink = jnp.exp2(old - new)
        m[rows, :] = new
        p = jnp.exp2(s[...] * SCALE - new[:, :1]).astype(BF16)
        r = dot(p, with_ones(kvb[kvi, :, D:]), NN)
        l[rows, :] = l[rows, :] * shrink + r[:, D:]
        acc[rows, :] = acc[rows, :] * shrink + r[:, :D]

    def attend(row0, n, kvi):
        @pl.when(n > 0)
        def _():
            scores(block(row0, 0), kvi, sa, ma)

            def pair(j, _):
                scores(block(row0, 2 * j + 1), kvi, sb, mb)
                absorb(block(row0, 2 * j), kvi, sa, ma)
                scores(block(row0, jnp.minimum(2 * j + 2, n - 1)), kvi, sa, ma)
                absorb(block(row0, 2 * j + 1), kvi, sb, mb)
                return 0

            lax.fori_loop(0, n // 2, pair, 0)

    ends = []
    running = jnp.int32(0)
    for p in range(8):
        running = running + lengths_ref[p]
        ends.append(running)
    starts = [jnp.int32(0)] + ends[:-1]

    def small(qv, kv_value, mask, rows, m_ref, l_ref, acc_ref):
        s = jnp.where(mask, dot(qv, kv_value[:, :D], NT) * SCALE, NEG)
        old = m_ref[rows, :]
        new = jnp.maximum(old, jnp.max(s, axis=1, keepdims=True))
        shrink = jnp.exp2(old - new)
        p = jnp.where(mask, jnp.exp2(s - new[:, :1]), 0.0).astype(BF16)
        r = dot(p, with_ones(kv_value[:, D:]), NN)
        m_ref[rows, :] = new
        l_ref[rows, :] = l_ref[rows, :] * shrink + r[:, D:]
        acc_ref[rows, :] = acc_ref[rows, :] * shrink + r[:, :D]

    def stretch_block(i, _):
        rows = block(0, i)
        index = lax.broadcasted_iota(jnp.int32, (RB, 1), 0) + i * RB
        own = i < 4
        near = i < 8
        home_zh = jnp.where(own, zh, jnp.where(near, zh + jnp.where(is_pre, 3, 1), zh + 2))
        home_zh = lax.rem(home_zh, 4)
        local = jnp.where(own, 0, jnp.where(near, 1024, jnp.where(is_pre, 2048 - half, 2048)))
        index = index - local
        place = (home_zh * 4 + y) * 128 + (index // 32) * 4 + lax.rem(index, 4)
        begin = jnp.zeros_like(place)
        for e in ends[:-1]:
            begin = jnp.where(place >= e, e, begin)
        keys = lax.broadcasted_iota(jnp.int32, (RB, half), 1) + zh * half
        mask = (keys >= begin) & (keys <= place)
        kv_value = strall[zh].reshape(half, 2 * D)
        small(qall[rows, :], kv_value, mask, rows, m, l, acc)
        return 0

    first_row = seq * 32

    def fresh_block(i, _):
        rows = block(0, i)
        index = lax.broadcasted_iota(jnp.int32, (RB, D), 0) + i * RB
        key = lax.broadcasted_iota(jnp.int32, (RB, D), 1)
        mask = (key // 4 == index // 32) & (lax.rem(key, 4) <= lax.rem(index, 4))
        small(qall[rows, :], new_ref[...], mask, rows, m, l, acc)
        return 0

    def cache_rows(g, _):
        for u in range(4):
            r = g * 4 + u
            rows = pl.ds(pl.multiple_of(r * 32, 32), 32)
            length = cache_len_ref[first_row + r]
            mask = lax.broadcasted_iota(jnp.int32, (32, half), 1) < length
            small(qall[rows, :], cacheb[r], mask, rows, m, l, acc)
        return 0

    def decode_first():
        lax.fori_loop(0, 1024 // RB, fresh_block, 0)
        for g in range(4):
            cache_copy(g).wait()
        lax.fori_loop(0, 4, cache_rows, 0)
        stretch_z.wait_recv()
        for c in stretch_y:
            c.start()
        for g in range(4, 8):
            cache_copy(g).wait()
        lax.fori_loop(4, 8, cache_rows, 0)

    def decode_last():
        for c in slab_copies:
            c.wait_recv()
        owner = lax.broadcasted_iota(jnp.int32, (256, 1), 0) // 32
        target = lax.rem(lax.broadcasted_iota(jnp.int32, (256, 1), 0), 32)
        for p in range(8):
            target = jnp.where(owner == p, target + (slots_ref[p] - first_row) * 32, target)
        chosen = lax.broadcasted_iota(jnp.int32, (256, 1024), 1) == target
        chosen = jnp.where(chosen, 1.0, 0.0).astype(BF16)
        pq[...] = dot(chosen, qall[pl.ds(0, 1024), :], NN).astype(BF16)
        pacc[...] = jnp.zeros_like(pacc)
        psum[...] = jnp.zeros_like(psum)
        pm[...] = jnp.full_like(pm, NEG)
        low = jnp.zeros_like(owner)
        high = jnp.zeros_like(owner)
        for p in range(8):
            low = jnp.where(owner == p, starts[p], low)
            high = jnp.where(owner == p, ends[p], high)

        def one(c, _):
            keys = lax.broadcasted_iota(jnp.int32, (256, half), 1) + c * half
            mask = (keys >= low) & (keys < high)
            small(pq[...], strall[c].reshape(half, 2 * D), mask, pl.ds(0, 256), pm, psum, pacc)
            return 0

        lax.fori_loop(0, 4, one, 0)

        total = psum[...]
        pm[...] = pm[...] + jnp.log2(total)
        pacc[...] = pacc[...] / total

        def merge(r, _):
            rows = pl.ds(pl.multiple_of(r * 32, 32), 32)
            other = jnp.full((32, D), NEG, F32)
            value = jnp.zeros((32, D), F32)
            for p in range(8):
                theirs = pl.ds(p * 32, 32)
                hit = jnp.full((32, D), slots_ref[p] - first_row - r, jnp.int32) == 0
                other = jnp.where(hit, pm[theirs, :], other)
                value = jnp.where(hit, pacc[theirs, :], value)
            old = m[rows, :]
            new = jnp.maximum(old, other)
            w0 = jnp.exp2(old - new)
            w1 = jnp.exp2(other - new)
            mixed = acc[rows, :] * w0 + value * w1
            out_ref[rows, :] = (mixed / (l[rows, :] * w0 + w1)).astype(BF16)
            return 0

        lax.fori_loop(0, 32, merge, 0)

    near_o, far_o = ob.at[pl.ds(0, 1024)], ob.at[pl.ds(1024, half)]
    o_copies_pre = [
        remote(far_o, ro.at[2, second], o_send.at[1], o_recv.at[3], 0, -4),
        remote(ls.at[1], rl.at[3], l_send.at[1], l_recv.at[3], 0, -4),
        remote(near_o, ro.at[1], o_send.at[0], o_recv.at[1], 0, -2),
        remote(ls.at[0], rl.at[1], l_send.at[0], l_recv.at[1], 0, -2),
    ]
    o_copies_dec = [
        remote(far_o, ro.at[2, first], o_send.at[1], o_recv.at[2], 0, 3),
        remote(ls.at[1], rl.at[2], l_send.at[1], l_recv.at[2], 0, 3),
        remote(near_o, ro.at[0], o_send.at[0], o_recv.at[0], 0, 1),
        remote(ls.at[0], rl.at[0], l_send.at[0], l_recv.at[0], 0, 1),
    ]

    def finish_block(b, _):
        rows = pl.ds(pl.multiple_of(1024 + b * D, D), D)
        total = l[rows, :]
        ob[pl.ds(pl.multiple_of(b * D, D), D), :] = (acc[rows, :] / total).astype(BF16)
        stat = jnp.transpose(m[rows, :] + jnp.log2(total))
        ls[b // 8, pl.ds(lax.rem(b, 8), 1), :] = stat[:1, :]
        return 0

    def send_results():
        ls[1, pl.ds(4, 4), :] = jnp.zeros((4, D), F32)
        lax.fori_loop(8, 12, finish_block, 0)

        @pl.when(is_pre)
        def _():
            for c in o_copies_pre[:2]:
                c.start()

        @pl.when(is_dec)
        def _():
            for c in o_copies_dec[:2]:
                c.start()

        lax.fori_loop(0, 8, finish_block, 0)

        @pl.when(is_pre)
        def _():
            for c in o_copies_pre[2:]:
                c.start()

        @pl.when(is_dec)
        def _():
            for c in o_copies_dec[2:]:
                c.start()

    def combine():
        for c in (o_copies_dec[2], o_copies_dec[3], o_copies_pre[2], o_copies_pre[3],
                  o_copies_dec[0], o_copies_dec[1], o_copies_pre[0], o_copies_pre[1]):
            c.wait_recv()

        def one(b, _):
            rows = pl.ds(pl.multiple_of(b * D, D), D)
            total = l[rows, :]
            stats = [m[rows, :] + jnp.log2(total)]
            values = [acc[rows, :] / total]
            for i in range(3):
                if i < 2:
                    row = rl[i, pl.ds(b, 1), :]
                else:
                    row = rl[2 + b // 4, pl.ds(lax.rem(b, 4), 1), :]
                stats.append(column(row))
                values.append(ro[i, rows, :].astype(F32))
            top = functools.reduce(jnp.maximum, stats)
            weights = [jnp.exp2(x - top) for x in stats]
            mixed = functools.reduce(jnp.add, [w * v for w, v in zip(weights, values)])
            out_ref[rows, :] = (mixed / functools.reduce(jnp.add, weights)).astype(BF16)
            return 0

        lax.fori_loop(0, 8, one, 0)

    def step(i, _):
        @pl.when(i == 1)
        def _():
            for c in kv_copies[:2]:
                c.wait_recv()
            for c in kv_copies[4:]:
                c.start()

        @pl.when(i == 2)
        def _():
            q_copies[0].wait_recv()
            q_copies[2].wait_recv()

        @pl.when(i == 4)
        def _():
            for c in kv_copies[2:4]:
                c.wait_recv()

        @pl.when(i == 5)
        def _():
            for c in kv_copies[4:]:
                c.wait_recv()

        @pl.when((i == 0) & is_dec)
        def _():
            decode_first()

        kvi = jnp.where(i < 2, i, jnp.where(i < 4, i - 2, jnp.where(i == 4, 2, 3)))
        only_own = (i < 2) | (i == 6)
        everything = (i == 4) & is_pre
        row0 = jnp.where(only_own | everything, 0, 1024)
        n_own = jnp.where(is_pre, 1024 // RB, 0)
        n = jnp.where(only_own, n_own, jnp.where(everything, 2560 // RB, 1536 // RB))
        attend(row0, n, kvi)

        @pl.when(i == 2)
        def _():
            for c in stretch_y:
                c.wait_recv()

            @pl.when(is_dec)
            def _():
                for c in slab_copies:
                    c.start()

        @pl.when(i == 3)
        def _():
            lax.fori_loop(jnp.where(is_pre, 0, 1024 // RB), 2560 // RB, stretch_block, 0)

        @pl.when(i == 5)
        def _():
            send_results()

        return 0

    lax.fori_loop(0, 7, step, 0)

    @pl.when(is_pre)
    def _():
        combine()

    @pl.when(is_dec)
    def _():
        decode_last()

    for c in kv_copies + stretch_y:
        c.wait_send()

    @pl.when(is_pre)
    def _():
        for c in [stretch_z] + q_copies + o_copies_pre:
            c.wait_send()

    @pl.when(is_dec)
    def _():
        for c in slab_copies + o_copies_dec:
            c.wait_send()


def body(queries, new_kv, prefix_kv, cache_kv, prompt_lengths, cache_lengths, prompt_slots):
    q = queries.reshape(32, 4, 8, D).transpose(0, 2, 1, 3).reshape(1024, D)
    new = new_kv.reshape(128, 2 * D)
    prefix = prefix_kv.reshape(1024, 2 * D)
    cache = cache_kv.reshape(32, 512, 2 * D)
    smem = pl.BlockSpec(memory_space=pltpu.SMEM)
    vmem = pl.BlockSpec(memory_space=pltpu.VMEM)
    hbm = pl.BlockSpec(memory_space=pl.ANY)
    dma = pltpu.SemaphoreType.DMA
    out = pl.pallas_call(
        kernel,
        out_shape=jax.ShapeDtypeStruct((1024, D), BF16),
        in_specs=[smem, smem, smem, hbm, vmem, hbm, hbm],
        out_specs=vmem,
        scratch_shapes=[
            pltpu.VMEM((4, 1024, 2 * D), BF16),
            pltpu.VMEM((2560, D), BF16),
            pltpu.VMEM((4, 4, 128, 2 * D), BF16),
            pltpu.VMEM((2560, D), F32),
            pltpu.VMEM((2560, D), F32),
            pltpu.VMEM((2560, D), F32),
            pltpu.VMEM((1536, D), BF16),
            pltpu.VMEM((2, 8, D), F32),
            pltpu.VMEM((3, 1024, D), BF16),
            pltpu.VMEM((4, 8, D), F32),
            pltpu.VMEM((32, 512, 2 * D), BF16),
            pltpu.VMEM((RB, 1024), F32),
            pltpu.VMEM((RB, 1024), F32),
            pltpu.VMEM((RB, D), F32),
            pltpu.VMEM((RB, D), F32),
            pltpu.VMEM((256, D), BF16),
            pltpu.VMEM((256, D), F32),
            pltpu.VMEM((256, D), F32),
            pltpu.VMEM((256, D), F32),
            dma((2,)), dma((8,)), dma((6,)), dma((6,)), dma((4,)), dma((2,)),
            dma((4,)), dma((4,)), dma((3,)), dma((3,)), dma((2,)), dma((4,)),
            dma((2,)), dma((4,)),
        ],
        compiler_params=pltpu.CompilerParams(
            collective_id=0, has_side_effects=True, vmem_limit_bytes=48 * 2**20
        ),
        cost_estimate=pl.CostEstimate(flops=10**10, bytes_accessed=10**7, transcendentals=10**7),
    )(prompt_lengths, cache_lengths, prompt_slots, q, new, prefix, cache)
    return out.reshape(32, 8, 4, D).transpose(0, 2, 1, 3).reshape(1, 128, 1024)


def solution(mesh):
    return jax.shard_map(
        body,
        mesh=mesh,
        in_specs=(
            P("role", "seq", "tensor"),
            P("role", "seq", "tensor", None),
            P("seq", "tensor", None),
            P("seq", None, "tensor", None),
            P(),
            P(),
            P(),
        ),
        out_specs=P("role", "seq", "tensor"),
        check_vma=False,
    )
```

time: 283 us -> 65.9 us (0.23)
  the two profiles are of different devices: /device:TPU:65 before, /device:TPU:4 now
where the time goes in v1:
time: 65.9 us; the launch traced here: 65.7 us
  Pallas kernels  59.8 us (91%)
  local copies, waits for them, and re-layouts  5.82 us (9%)
    pallas_call x1, Pallas kernels, body(): pl.pallas_call(kernel, out_shape=jax.ShapeDtypeStruct((1024, D), BF16), i...  59.8 us
    unnamed x11, local copies, waits for them, and re-layouts  4.86 us

profile of v1, /device:TPU:4, one launch (start us, length us, event | category | flops | bytes accessed | tf_op | source)
XLA Modules:
  0.0 65.7 jit_solution(2748671636756751527)
XLA Ops:
  0.0 1.0 %copy.10 = bf16[16,8,8,128]{3,2,1,0:T(8,128)(2,1)S(1)} copy(bf16[16,8,8,128]{3,1,2,0:T(8,128)(2,1)} %bitcast.20) | data formatting | bytes 524288
  1.0 0.1 copy.8
  1.1 0.0 copy-start
  1.1 1.0 %copy-done = bf16[1024,1,256]{2,0,1:T(8,128)(2,1)S(1)} copy-done((bf16[1024,1,256]{2,0,1:T(8,128)(2,1)S(1)}, bf16[1024,1,256]{2,0,1:T(8,128)(2,1)}, u32[]{:S(2)}) %copy-start) | copy-done | bytes 524312
  2.2 0.0 copy-start.1
  2.2 0.8 %copy-done.1 = bf16[1,128,1,256]{3,1,2,0:T(8,128)(2,1)S(1)} copy-done((bf16[1,128,1,256]{3,1,2,0:T(8,128)(2,1)S(1)}, bf16[1,128,1,256]{3,1,2,0:T(8,128)(2,1)}, u32[]{:S(2)}) %copy-start.1) | copy-done | bytes 65560
  3.0 0.0 copy-start.2
  3.0 0.7 %copy-done.2 = s32[512]{0:T(512)S(1)} copy-done((s32[512]{0:T(512)S(1)}, s32[512]{0:T(512)}, u32[]{:S(2)}) %copy-start.2) | copy-done | bytes 2072
  3.7 0.0 copy-start.3
  3.7 0.7 copy-done.3
  4.3 0.0 copy-start.4
  4.3 0.7 copy-done.4
  5.0 59.8 %shard_map.73 = bf16[1024,128]{1,0:T(8,128)(2,1)S(1)} custom-call(s32[8]{0:T(128)S(1)} %copy-done.3, s32[512]{0:T(512)S(1)} %copy-done.2, s32[8]{0:T(128)S(1)} %copy-done.4, bf16[1024,128]{1,0:T(8,128)(2,1)S(1)} %bitcast.15, bf16[128,256]{1,0:T(8,128)(2,1)S(1)} %bitcast.18, bf16[1024,256]{1,0:T(8,128)(2,1)S(1)} %bitcast.17, bf16[32,512,256]{2,1,0:T(8,128)(2,1)} %bitcast.21), custom_call_target="tpu_custom_call" | custom-call | flops 10000000000 | bytes 10000000 | tf_op jit(solution)/shard_map/pallas_call | solution.py:445
  64.9 0.8 %reshape.27 = bf16[1,128,1024]{2,1,0:T(8,128)(2,1)} reshape(bf16[32,4,8,128]{3,2,1,0:T(8,128)(2,1)S(1)} %copy.9) | data formatting | bytes 524288 | tf_op jit(solution)/shard_map/reshape | solution.py:479
  (1 shorter events, 0.0 us)
Async XLA Ops:
  1.1 1.0 %copy-start = (bf16[1024,1,256]{2,0,1:T(8,128)(2,1)S(1)}, bf16[1024,1,256]{2,0,1:T(8,128)(2,1)}, u32[]{:S(2)}) copy-start(bf16[1024,1,256]{2,0,1:T(8,128)(2,1)} %param.9) | copy-start | bytes 1572868
  2.2 0.8 %copy-start.1 = (bf16[1,128,1,256]{3,1,2,0:T(8,128)(2,1)S(1)}, bf16[1,128,1,256]{3,1,2,0:T(8,128)(2,1)}, u32[]{:S(2)}) copy-start(bf16[1,128,1,256]{3,1,2,0:T(8,128)(2,1)} %param.8) | copy-start | bytes 196612
  3.0 0.7 %copy-start.2 = (s32[512]{0:T(512)S(1)}, s32[512]{0:T(512)}, u32[]{:S(2)}) copy-start(s32[512]{0:T(512)} %cache_len_ref.1) | copy-start | bytes 6148
  3.7 0.7 copy-start.3
  4.3 0.7 copy-start.4

commit v2 on v1

v2 whole, which is shorter than its diff:
```python
import functools
import math

import jax
import jax.numpy as jnp
from jax import lax
from jax.experimental import pallas as pl
from jax.experimental.pallas import tpu as pltpu
from jax.sharding import PartitionSpec as P

MESH = pl.DeviceIdType.MESH
NEG = -1e30
D = 128
SCALE = math.log2(math.e) / math.sqrt(D)
RB = 256
NT = (((1,), (1,)), ((), ()))
NN = (((1,), (0,)), ((), ()))
F32 = jnp.float32
BF16 = jnp.bfloat16


def dot(a, b, dims):
    return lax.dot_general(a, b, dims, preferred_element_type=F32)


def with_ones(v):
    return jnp.concatenate([v, jnp.ones_like(v)], axis=1)


def column(row):
    return jnp.transpose(jnp.broadcast_to(row, (D, D)))


def kernel(
    lengths_hbm, cache_len_hbm, slots_hbm, q_ref, new_hbm, prefix_ref, cache_ref,
    out_ref,
    kvb, qall, acc, m, l, ob, ls, ro, rl, rof, rlf, cacheb, sa, sb, ma, mb,
    pqall, pacc, pm, psum, pob, pls, pback, plback, new_ref, lengths_ref, cache_len_ref, slots_ref,
    local_sem, cache_sem, kv_send, kv_recv, q_send, q_recv, str_send, str_recv,
    p_send, p_recv, pb_send, pb_recv, o_send, o_recv, l_send, l_recv,
):
    role = lax.axis_index("role")
    seq = lax.axis_index("seq")
    tensor = lax.axis_index("tensor")
    zh, y = seq // 4, lax.rem(seq, 4)
    z = zh * 2 + role

    def dev(dy, dz):
        yy = lax.rem(y + dy + 8, 4)
        zz = lax.rem(z + dz + 8, 8)
        return (lax.rem(zz, 2), (zz // 2) * 4 + yy, tensor)

    def remote(src, dst, ss, rs, dy, dz):
        return pltpu.make_async_remote_copy(
            src_ref=src, dst_ref=dst, send_sem=ss, recv_sem=rs,
            device_id=dev(dy, dz), device_id_type=MESH,
        )

    is_pre = role == 0
    is_dec = role == 1
    half = 512

    own_kv = pltpu.make_async_copy(prefix_ref, kvb.at[pl.ds(0, 1024)], local_sem.at[0])
    own_kv.start()
    own_q = pltpu.make_async_copy(q_ref, qall.at[pl.ds(0, 1024)], local_sem.at[1])
    own_q.start()
    own_new = pltpu.make_async_copy(new_hbm, new_ref, local_sem.at[2])
    own_new.start()
    scalars = [
        pltpu.make_async_copy(lengths_hbm, lengths_ref, local_sem.at[3]),
        pltpu.make_async_copy(cache_len_hbm, cache_len_ref, local_sem.at[4]),
        pltpu.make_async_copy(slots_hbm, slots_ref, local_sem.at[5]),
    ]
    for c in scalars:
        c.start()

    def cache_copy(g):
        rows = pl.ds(g * 4, 4)
        return pltpu.make_async_copy(cache_ref.at[rows], cacheb.at[rows], cache_sem.at[g])

    @pl.when(is_dec)
    def _():
        for g in range(8):
            cache_copy(g).start()

    barrier = pltpu.get_barrier_semaphore()
    peers = [(0, dz) for dz in (1, 2, 4, 6, 7)] + [(1, 0), (2, 0), (3, 0)]
    for dy, dz in peers:
        pl.semaphore_signal(barrier, inc=1, device_id=dev(dy, dz), device_id_type=MESH)
    def clear(b, _):
        rows = pl.ds(pl.multiple_of(b * D, D), D)
        acc[rows, :] = jnp.zeros((D, D), F32)
        l[rows, :] = jnp.zeros((D, D), F32)
        m[rows, :] = jnp.full((D, D), NEG, F32)
        return 0

    lax.fori_loop(0, 20, clear, 0)

    own_kv.wait()
    own_new.wait()
    own_q.wait()
    for c in scalars:
        c.wait()
    pl.semaphore_wait(barrier, len(peers))

    own_stretch = pl.ds(pl.multiple_of(2 * 1024 + y * 128, 128), 128)
    slot = kvb.at[own_stretch]
    stretch_y = [remote(slot, slot, str_send.at[i], str_recv.at[i], dy, 0) for i, dy in enumerate((1, 3, 2))]
    stretch_z = remote(slot, slot, str_send.at[3], str_recv.at[3], 0, 1)
    def part(piece, h):
        return kvb.at[pl.ds((0, 1024, 2560, 3584)[piece] + h * half, half)]

    kv_copies = [
        remote(part(0, 0), part(1, 0), kv_send.at[0], kv_recv.at[0], 1, 0),
        remote(part(0, 1), part(1, 1), kv_send.at[1], kv_recv.at[1], 3, 0),
        remote(part(0, 1), part(2, 0), kv_send.at[2], kv_recv.at[2], 1, 0),
        remote(part(0, 0), part(2, 1), kv_send.at[3], kv_recv.at[3], 3, 0),
        remote(part(1, 0), part(3, 0), kv_send.at[4], kv_recv.at[4], 1, 0),
        remote(part(1, 1), part(3, 1), kv_send.at[5], kv_recv.at[5], 3, 0),
    ]
    home_q, near_q = qall.at[pl.ds(0, 1024)], qall.at[pl.ds(1024, 1024)]
    far_q = qall.at[pl.ds(2048, half)]
    q_copies = [
        remote(home_q, near_q, q_send.at[0], q_recv.at[0], 0, -1),
        remote(home_q, near_q, q_send.at[1], q_recv.at[0], 0, 2),
    ]
    far_q_pre = remote(qall.at[pl.ds(1024 + half, half)], far_q, q_send.at[2], q_recv.at[1], 0, 2)
    far_q_dec = remote(qall.at[pl.ds(1024, half)], far_q, q_send.at[2], q_recv.at[1], 0, -2)
    p_copies = [
        remote(pqall.at[0], pqall.at[d], p_send.at[d - 1], p_recv.at[d - 1], 0, 2 * d) for d in (1, 2, 3)
    ]
    p_back = []
    for d in (1, 2, 3):
        p_back.append(remote(pob.at[d], pback.at[d], pb_send.at[d - 1, 0], pb_recv.at[d - 1, 0], 0, -2 * d))
        p_back.append(remote(pls.at[d], plback.at[d], pb_send.at[d - 1, 1], pb_recv.at[d - 1, 1], 0, -2 * d))

    @pl.when(is_pre)
    def _():
        kvb[own_stretch, :] = new_ref[...]
        stretch_z.start()
        for c in stretch_y:
            c.start()

    for c in kv_copies[:4]:
        c.start()

    @pl.when(is_pre)
    def _():
        for c in q_copies:
            c.start()

    def block(row0, i):
        return pl.ds(pl.multiple_of(row0 + i * RB, RB), RB)

    def scores(b, k0, span, masked, s, mx):
        rows = block(0, b)
        x = dot(qall[rows, :], kvb[pl.ds(k0, span), :D], NT)
        s[:, :span] = x
        if masked is None:
            top = jnp.max(x, axis=1, keepdims=True)
        else:
            begin, place = stretch_range(b)
            keys = lax.broadcasted_iota(jnp.int32, (RB, half), 1) + zh * half
            y0 = jnp.where((keys >= begin) & (keys <= place), x[:, masked : masked + half], NEG)
            s[:, masked : masked + half] = y0
            top = jnp.maximum(
                jnp.max(x[:, :masked], axis=1, keepdims=True), jnp.max(y0, axis=1, keepdims=True)
            )
            if masked + half < span:
                top = jnp.maximum(top, jnp.max(x[:, masked + half :], axis=1, keepdims=True))
        mx[...] = jnp.broadcast_to(top * SCALE, mx.shape)

    def absorb(b, k0, span, s, mx):
        rows = block(0, b)
        old = m[rows, :]
        new = jnp.maximum(old, mx[...])
        shrink = jnp.exp2(old - new)
        m[rows, :] = new
        p = jnp.exp2(s[:, :span] * SCALE - new[:, :1]).astype(BF16)
        r = dot(p, with_ones(kvb[pl.ds(k0, span), D:]), NN)
        l[rows, :] = l[rows, :] * shrink + r[:, D:]
        acc[rows, :] = acc[rows, :] * shrink + r[:, :D]

    def attend(b0, n, k0, span, masked=None):
        scores(b0, k0, span, masked, sa, ma)

        def pair(j, _):
            b = b0 + 2 * j
            scores(b + 1, k0, span, masked, sb, mb)
            absorb(b, k0, span, sa, ma)
            scores(jnp.minimum(b + 2, b0 + n - 1), k0, span, masked, sa, ma)
            absorb(b + 1, k0, span, sb, mb)
            return 0

        lax.fori_loop(0, n // 2, pair, 0)

    def weigh(stats, values):
        top = functools.reduce(jnp.maximum, stats)
        weights = [jnp.exp2(x - top) for x in stats]
        total = functools.reduce(jnp.add, weights)
        mixed = functools.reduce(jnp.add, [w * v for w, v in zip(weights, values)])
        return mixed / total, top + jnp.log2(total)

    ends = []
    running = jnp.int32(0)
    for p in range(8):
        running = running + lengths_ref[p]
        ends.append(running)
    starts = [jnp.int32(0)] + ends[:-1]

    def small(qv, kv_value, mask, rows, m_ref, l_ref, acc_ref):
        s = jnp.where(mask, dot(qv, kv_value[:, :D], NT) * SCALE, NEG)
        old = m_ref[rows, :]
        new = jnp.maximum(old, jnp.max(s, axis=1, keepdims=True))
        shrink = jnp.exp2(old - new)
        p = jnp.exp2(s - new[:, :1]).astype(BF16)
        r = dot(p, with_ones(kv_value[:, D:]), NN)
        m_ref[rows, :] = new
        l_ref[rows, :] = l_ref[rows, :] * shrink + r[:, D:]
        acc_ref[rows, :] = acc_ref[rows, :] * shrink + r[:, :D]

    def stretch_range(i):
        index = lax.broadcasted_iota(jnp.int32, (RB, 1), 0) + i * RB
        own = i < 4
        near = i < 8
        home_zh = jnp.where(own, zh, jnp.where(near, zh + jnp.where(is_pre, 3, 1), zh + 2))
        home_zh = lax.rem(home_zh, 4)
        index = index - jnp.where(own, 0, jnp.where(near, 1024, jnp.where(is_pre, 2048 - half, 2048)))
        place = (home_zh * 4 + y) * 128 + (index // 32) * 4 + lax.rem(index, 4)
        begin = jnp.zeros_like(place)
        for e in ends[:-1]:
            begin = jnp.where(place >= e, e, begin)
        return begin, place

    first_row = seq * 32

    def fresh_block(i, _):
        rows = block(0, i)
        index = lax.broadcasted_iota(jnp.int32, (RB, D), 0) + i * RB
        key = lax.broadcasted_iota(jnp.int32, (RB, D), 1)
        mask = (key // 4 == index // 32) & (lax.rem(key, 4) <= lax.rem(index, 4))
        small(qall[rows, :], new_ref[...], mask, rows, m, l, acc)
        return 0

    def cache_rows(g, _):
        for u in range(4):
            r = g * 4 + u
            rows = pl.ds(pl.multiple_of(r * 32, 32), 32)
            length = cache_len_ref[first_row + r]
            mask = lax.broadcasted_iota(jnp.int32, (32, half), 1) < length
            small(qall[rows, :], cacheb[r], mask, rows, m, l, acc)
        return 0

    def decode_first():
        owner = lax.broadcasted_iota(jnp.int32, (256, 1), 0) // 32
        target = lax.rem(lax.broadcasted_iota(jnp.int32, (256, 1), 0), 32)
        for p in range(8):
            target = jnp.where(owner == p, target + (slots_ref[p] - first_row) * 32, target)
        chosen = lax.broadcasted_iota(jnp.int32, (256, 1024), 1) == target
        chosen = jnp.where(chosen, 1.0, 0.0).astype(BF16)
        pqall[0] = dot(chosen, qall[pl.ds(0, 1024), :], NN).astype(BF16)
        for c in p_copies:
            c.start()
        lax.fori_loop(0, 1024 // RB, fresh_block, 0)
        for g in range(4):
            cache_copy(g).wait()
        lax.fori_loop(0, 4, cache_rows, 0)
        stretch_z.wait_recv()
        for c in stretch_y:
            c.start()
        for g in range(4, 8):
            cache_copy(g).wait()
        lax.fori_loop(4, 8, cache_rows, 0)

    def prompt_part():
        for c in p_copies:
            c.wait_recv()
        pacc[...] = jnp.zeros_like(pacc)
        psum[...] = jnp.zeros_like(psum)
        pm[...] = jnp.full_like(pm, NEG)
        owner = lax.broadcasted_iota(jnp.int32, (256, 1), 0) // 32
        low = jnp.zeros_like(owner)
        high = jnp.zeros_like(owner)
        for p in range(8):
            low = jnp.where(owner == p, starts[p], low)
            high = jnp.where(owner == p, ends[p], high)
        keys = lax.broadcasted_iota(jnp.int32, (256, half), 1) + zh * half
        mask = (keys >= low) & (keys < high)

        def one(d, _):
            rows = block(0, d)
            small(pqall[d], kvb[pl.ds(2048, half), :], mask, rows, pm, psum, pacc)
            total = psum[rows, :]
            pob[d] = (pacc[rows, :] / total).astype(BF16)
            stat = pm[rows, :] + jnp.log2(total)
            pls[d] = jnp.zeros((8, D), F32)
            pls[d, pl.ds(0, 1), :] = jnp.transpose(stat[:D])[:1]
            pls[d, pl.ds(1, 1), :] = jnp.transpose(stat[D:])[:1]
            return 0

        lax.fori_loop(0, 4, one, 0)
        for c in p_back:
            c.start()

    def decode_last():
        for c in p_back:
            c.wait_recv()
        pback[0] = pob[0]
        plback[0] = pls[0]
        for b in range(2):
            rows = pl.ds(b * D, D)
            mixed, stat = weigh(
                [column(plback[d, pl.ds(b, 1), :]) for d in range(4)],
                [pback[d, rows, :].astype(F32) for d in range(4)],
            )
            pm[rows, :] = stat
            pacc[rows, :] = mixed

        def merge(r, _):
            rows = pl.ds(pl.multiple_of(r * 32, 32), 32)
            other = jnp.full((32, D), NEG, F32)
            value = jnp.zeros((32, D), F32)
            for p in range(8):
                theirs = pl.ds(p * 32, 32)
                hit = jnp.full((32, D), slots_ref[p] - first_row - r, jnp.int32) == 0
                other = jnp.where(hit, pm[theirs, :], other)
                value = jnp.where(hit, pacc[theirs, :], value)
            old = m[rows, :]
            new = jnp.maximum(old, other)
            w0 = jnp.exp2(old - new)
            w1 = jnp.exp2(other - new)
            mixed = acc[rows, :] * w0 + value * w1
            out_ref[rows, :] = (mixed / (l[rows, :] * w0 + w1)).astype(BF16)
            return 0

        lax.fori_loop(0, 32, merge, 0)

    far_o = ob.at[pl.ds(1024, half)]
    far_pre = [
        remote(far_o, rof, o_send.at[0], o_recv.at[0], 0, -2),
        remote(ls.at[2], rlf, l_send.at[0], l_recv.at[0], 0, -2),
    ]
    far_dec = [
        remote(far_o, rof, o_send.at[0], o_recv.at[0], 0, 2),
        remote(ls.at[2], rlf, l_send.at[0], l_recv.at[0], 0, 2),
    ]
    near_pre, near_dec = [], []
    for h in range(2):
        rows = pl.ds(h * half, half)
        near_pre.append([
            remote(ob.at[rows], ro.at[1, rows], o_send.at[1 + h], o_recv.at[3 + h], 0, -2),
            remote(ls.at[h], rl.at[1, h], l_send.at[1 + h], l_recv.at[3 + h], 0, -2),
        ])
        near_dec.append([
            remote(ob.at[rows], ro.at[0, rows], o_send.at[1 + h], o_recv.at[1 + h], 0, 1),
            remote(ls.at[h], rl.at[0, h], l_send.at[1 + h], l_recv.at[1 + h], 0, 1),
        ])

    def start_all(pre, dec):
        @pl.when(is_pre)
        def _():
            for c in pre:
                c.start()

        @pl.when(is_dec)
        def _():
            for c in dec:
                c.start()

    def finish_block(b, _):
        rows = pl.ds(pl.multiple_of(1024 + b * D, D), D)
        total = l[rows, :]
        ob[pl.ds(pl.multiple_of(b * D, D), D), :] = (acc[rows, :] / total).astype(BF16)
        stat = jnp.transpose(m[rows, :] + jnp.log2(total))
        ls[b // 4, pl.ds(lax.rem(b, 4), 1), :] = stat[:1, :]
        return 0

    def merge_block(b, _):
        rows = pl.ds(pl.multiple_of(1024 + b * D, D), D)
        theirs = lax.rem(b, 4)
        total = l[rows, :]
        mixed, stat = weigh(
            [m[rows, :] + jnp.log2(total), column(rlf[pl.ds(theirs, 1), :])],
            [acc[rows, :] / total, rof[pl.ds(pl.multiple_of(theirs * D, D), D), :].astype(F32)],
        )
        ob[pl.ds(pl.multiple_of(b * D, D), D), :] = mixed.astype(BF16)
        ls[b // 4, pl.ds(theirs, 1), :] = jnp.transpose(stat)[:1, :]
        return 0

    def send_far():
        ls[...] = jnp.zeros_like(ls)
        lax.fori_loop(8, 12, finish_block, 0)
        start_all(far_pre, far_dec)

    def send_near():
        first_block = jnp.where(is_pre, 0, 4)
        lax.fori_loop(first_block, first_block + 4, finish_block, 0)
        start_all(near_pre[0], near_dec[1])

    def send_merged():
        for c in far_pre:
            c.wait_recv()
        first_block = jnp.where(is_pre, 4, 0)
        lax.fori_loop(first_block, first_block + 4, merge_block, 0)
        start_all(near_pre[1], near_dec[0])

    def combine():
        for c in near_dec[1] + near_pre[0] + near_dec[0] + near_pre[1]:
            c.wait_recv()

        def one(b, _):
            rows = pl.ds(pl.multiple_of(b * D, D), D)
            total = l[rows, :]
            stats = [m[rows, :] + jnp.log2(total)]
            values = [acc[rows, :] / total]
            for i in range(2):
                stats.append(column(rl[i, b // 4, pl.ds(lax.rem(b, 4), 1), :]))
                values.append(ro[i, rows, :].astype(F32))
            mixed, _ = weigh(stats, values)
            out_ref[rows, :] = mixed.astype(BF16)
            return 0

        lax.fori_loop(0, 8, one, 0)

    @pl.when(is_pre)
    def _():
        attend(0, 4, 0, 1024)

    @pl.when(is_dec)
    def _():
        decode_first()

    for c in kv_copies[:2]:
        c.wait_recv()
    for c in kv_copies[4:]:
        c.start()
    q_copies[0].wait_recv()
    start_all([far_q_pre], [far_q_dec])
    for c in stretch_y:
        c.wait_recv()

    def wide(i, _):
        @pl.when(i == 1)
        def _():
            far_q_pre.wait_recv()

        attend(4 + 4 * i, 4 - 2 * i, 0, 2560, 2048)
        return 0

    lax.fori_loop(0, 2, wide, 0)

    @pl.when(is_dec)
    def _():
        prompt_part()

    def narrow(i, _):
        @pl.when(i == 0)
        def _():
            for c in kv_copies[2:4]:
                c.wait_recv()

        @pl.when(i == 1)
        def _():
            for c in kv_copies[4:]:
                c.wait_recv()

        attend(
            jnp.where(i == 1, 8, 4),
            jnp.where(i == 0, 6, jnp.where(i == 1, 2, 4)),
            pl.multiple_of(jnp.where(i == 0, 2560, 3584), half),
            1024,
        )

        @pl.when(i == 1)
        def _():
            send_far()

        return 0

    lax.fori_loop(0, 3, narrow, 0)
    send_near()

    def rest(i, _):
        @pl.when(is_pre)
        def _():
            attend(2 * i, 2, 1024, 3584, 1024)

        @pl.when(i == 0)
        def _():
            send_merged()

        return 0

    lax.fori_loop(0, 2, rest, 0)

    @pl.when(is_pre)
    def _():
        combine()

    @pl.when(is_dec)
    def _():
        decode_last()

    for c in kv_copies + stretch_y + [far_q_pre] + far_pre + near_pre[0] + near_pre[1]:
        c.wait_send()

    @pl.when(is_pre)
    def _():
        for c in [stretch_z] + q_copies:
            c.wait_send()

    @pl.when(is_dec)
    def _():
        for c in p_copies + p_back:
            c.wait_send()


def body(queries, new_kv, prefix_kv, cache_kv, prompt_lengths, cache_lengths, prompt_slots):
    q = queries.reshape(32, 4, 8, D).transpose(0, 2, 1, 3).reshape(1024, D)
    new = new_kv.reshape(128, 2 * D)
    prefix = prefix_kv.reshape(1024, 2 * D)
    cache = cache_kv.reshape(32, 512, 2 * D)
    vmem = pl.BlockSpec(memory_space=pltpu.VMEM)
    hbm = pl.BlockSpec(memory_space=pl.ANY)
    dma = pltpu.SemaphoreType.DMA
    out = pl.pallas_call(
        kernel,
        out_shape=jax.ShapeDtypeStruct((1024, D), BF16),
        in_specs=[hbm] * 7,
        out_specs=vmem,
        scratch_shapes=[
            pltpu.VMEM((4608, 2 * D), BF16),
            pltpu.VMEM((2560, D), BF16),
            pltpu.VMEM((2560, D), F32),
            pltpu.VMEM((2560, D), F32),
            pltpu.VMEM((2560, D), F32),
            pltpu.VMEM((1536, D), BF16),
            pltpu.VMEM((3, 8, D), F32),
            pltpu.VMEM((2, 1024, D), BF16),
            pltpu.VMEM((2, 2, 8, D), F32),
            pltpu.VMEM((512, D), BF16),
            pltpu.VMEM((8, D), F32),
            pltpu.VMEM((32, 512, 2 * D), BF16),
            pltpu.VMEM((RB, 3584), F32),
            pltpu.VMEM((RB, 3584), F32),
            pltpu.VMEM((RB, D), F32),
            pltpu.VMEM((RB, D), F32),
            pltpu.VMEM((4, 256, D), BF16),
            pltpu.VMEM((1024, D), F32),
            pltpu.VMEM((1024, D), F32),
            pltpu.VMEM((1024, D), F32),
            pltpu.VMEM((4, 256, D), BF16),
            pltpu.VMEM((4, 8, D), F32),
            pltpu.VMEM((4, 256, D), BF16),
            pltpu.VMEM((4, 8, D), F32),
            pltpu.VMEM((128, 2 * D), BF16),
            pltpu.SMEM((8,), jnp.int32),
            pltpu.SMEM((512,), jnp.int32),
            pltpu.SMEM((8,), jnp.int32),
            dma((6,)), dma((8,)), dma((6,)), dma((6,)), dma((3,)), dma((2,)),
            dma((4,)), dma((4,)), dma((3,)), dma((3,)), dma((3, 2)), dma((3, 2)),
            dma((3,)), dma((5,)), dma((3,)), dma((5,)),
        ],
        compiler_params=pltpu.CompilerParams(
            collective_id=0, has_side_effects=True, vmem_limit_bytes=62 * 2**20
        ),
        cost_estimate=pl.CostEstimate(flops=10**10, bytes_accessed=10**7, transcendentals=10**7),
    )(prompt_lengths, cache_lengths, prompt_slots, q, new, prefix, cache)
    return out.reshape(32, 8, 4, D).transpose(0, 2, 1, 3).reshape(1, 128, 1024)


def solution(mesh):
    return jax.shard_map(
        body,
        mesh=mesh,
        in_specs=(
            P("role", "seq", "tensor"),
            P("role", "seq", "tensor", None),
            P("seq", "tensor", None),
            P("seq", None, "tensor", None),
            P(),
            P(),
            P(),
        ),
        out_specs=P("role", "seq", "tensor"),
        check_vma=False,
    )
```

time: 65.9 us -> 58.4 us (0.89)
  Pallas kernels: 59.8 us -> 54.6 us
  local copies, waits for them, and re-layouts: 5.82 us -> 3.6 us
    pallas_call x1, Pallas kernels: 59.8 us -> 54.6 us  [body(): pl.pallas_call(kernel, out_shape=jax.ShapeDtypeStruct((1024, D), BF16), i...]
    unnamed x11 -> x1, local copies, waits for them, and re-layouts: 4.86 us -> 0.99 us
    transpose x1, local copies, waits for them, and re-layouts: 0.04 us -> 0.99 us  [body(): return out.reshape(32, 8, 4, D).transpose(0, 2, 1, 3).reshape(1, 128, 1024)]
    reshape x1, local copies, waits for them, and re-layouts: 0.1 us -> 0.81 us  [body(): q = queries.reshape(32, 4, 8, D).transpose(0, 2, 1, 3).reshape(1024, D)]
where the time goes in v2:
time: 58.4 us; the launch traced here: 58.2 us
  Pallas kernels  54.6 us (93%)
  local copies, waits for them, and re-layouts  3.6 us (6%)
    pallas_call x1, Pallas kernels, body(): pl.pallas_call(kernel, out_shape=jax.ShapeDtypeStruct((1024, D), BF16), i...  54.6 us

profile of v2, /device:TPU:4, one launch (start us, length us, event | category | flops | bytes accessed | tf_op | source)
XLA Modules:
  0.0 58.2 jit_solution(6125280394913565298)
XLA Ops:
  0.0 1.0 %copy.10 = bf16[16,8,8,128]{3,2,1,0:T(8,128)(2,1)S(1)} copy(bf16[16,8,8,128]{3,1,2,0:T(8,128)(2,1)} %bitcast.16) | data formatting | bytes 524288
  1.0 0.8 %copy.8 = bf16[32,4,8,128]{3,1,2,0:T(4,128)(2,1)} copy(bf16[32,4,8,128]{3,2,1,0:T(8,128)(2,1)S(1)} %bitcast.15) | data formatting | bytes 524288 | tf_op jit(solution)/shard_map/reshape | solution.py:519
  1.8 54.6 %shard_map.73 = bf16[1024,128]{1,0:T(8,128)(2,1)} custom-call(s32[8]{0:T(128)} %lengths_hbm.1, s32[512]{0:T(512)} %cache_len_hbm.1, s32[8]{0:T(128)} %slots_hbm.1, bf16[1024,128]{1,0:T(8,128)(2,1)} %bitcast.17, bf16[128,256]{1,0:T(8,128)(2,1)} %bitcast.21, bf16[1024,256]{1,0:T(8,128)(2,1)} %bitcast.20, bf16[32,512,256]{2,1,0:T(8,128)(2,1)} %bitcast.19), custom_call_target="tpu_custom_call" | custom-call | flops 10000000000 | bytes 10000000 | tf_op jit(solution)/shard_map/pallas_call | solution.py:526
  56.4 1.0 %copy.9 = bf16[32,4,8,128]{3,2,1,0:T(8,128)(2,1)S(1)} copy(bf16[32,4,8,128]{3,1,2,0:T(4,128)(2,1)} %bitcast.18) | data formatting | bytes 524288 | tf_op jit(solution)/shard_map/transpose | solution.py:569
  57.4 0.8 %reshape.27 = bf16[1,128,1024]{2,1,0:T(8,128)(2,1)} reshape(bf16[32,4,8,128]{3,2,1,0:T(8,128)(2,1)S(1)} %copy.9) | data formatting | bytes 524288 | tf_op jit(solution)/shard_map/reshape | solution.py:569

commit v3 on v2

--- a/solution.py
+++ b/solution.py
@@ -77,11 +77,6 @@
     def cache_copy(g):
         rows = pl.ds(g * 4, 4)
         return pltpu.make_async_copy(cache_ref.at[rows], cacheb.at[rows], cache_sem.at[g])
-
-    @pl.when(is_dec)
-    def _():
-        for g in range(8):
-            cache_copy(g).start()
 
     barrier = pltpu.get_barrier_semaphore()
     peers = [(0, dz) for dz in (1, 2, 4, 6, 7)] + [(1, 0), (2, 0), (3, 0)]
@@ -138,16 +133,19 @@
     def _():
         kvb[own_stretch, :] = new_ref[...]
         stretch_z.start()
-        for c in stretch_y:
-            c.start()
-
-    for c in kv_copies[:4]:
+
+    for c in kv_copies[:2]:
         c.start()
 
     @pl.when(is_pre)
     def _():
         for c in q_copies:
             c.start()
+
+    @pl.when(is_dec)
+    def _():
+        for g in range(8):
+            cache_copy(g).start()
 
     def block(row0, i):
         return pl.ds(pl.multiple_of(row0 + i * RB, RB), RB)
@@ -163,9 +161,9 @@
             keys = lax.broadcasted_iota(jnp.int32, (RB, half), 1) + zh * half
             y0 = jnp.where((keys >= begin) & (keys <= place), x[:, masked : masked + half], NEG)
             s[:, masked : masked + half] = y0
-            top = jnp.maximum(
-                jnp.max(x[:, :masked], axis=1, keepdims=True), jnp.max(y0, axis=1, keepdims=True)
-            )
+            top = jnp.max(y0, axis=1, keepdims=True)
+            if masked:
+                top = jnp.maximum(top, jnp.max(x[:, :masked], axis=1, keepdims=True))
             if masked + half < span:
                 top = jnp.maximum(top, jnp.max(x[:, masked + half :], axis=1, keepdims=True))
         mx[...] = jnp.broadcast_to(top * SCALE, mx.shape)
@@ -250,6 +248,12 @@
             mask = lax.broadcasted_iota(jnp.int32, (32, half), 1) < length
             small(qall[rows, :], cacheb[r], mask, rows, m, l, acc)
         return 0
+
+    def second_copies():
+        for c in kv_copies[:2]:
+            c.wait_send()
+        for c in stretch_y + kv_copies[2:4]:
+            c.start()
 
     def decode_first():
         owner = lax.broadcasted_iota(jnp.int32, (256, 1), 0) // 32
@@ -266,8 +270,7 @@
             cache_copy(g).wait()
         lax.fori_loop(0, 4, cache_rows, 0)
         stretch_z.wait_recv()
-        for c in stretch_y:
-            c.start()
+        second_copies()
         for g in range(4, 8):
             cache_copy(g).wait()
         lax.fori_loop(4, 8, cache_rows, 0)
@@ -425,6 +428,7 @@
     @pl.when(is_pre)
     def _():
         attend(0, 4, 0, 1024)
+        second_copies()
 
     @pl.when(is_dec)
     def _():
@@ -432,53 +436,41 @@
 
     for c in kv_copies[:2]:
         c.wait_recv()
-    for c in kv_copies[4:]:
-        c.start()
     q_copies[0].wait_recv()
     start_all([far_q_pre], [far_q_dec])
-    for c in stretch_y:
-        c.wait_recv()
 
     def wide(i, _):
         @pl.when(i == 1)
         def _():
+            for c in kv_copies[4:]:
+                c.start()
             far_q_pre.wait_recv()
 
-        attend(4 + 4 * i, 4 - 2 * i, 0, 2560, 2048)
+        attend(4 + 4 * i, 4 - 2 * i, 0, 2048)
         return 0
 
     lax.fori_loop(0, 2, wide, 0)
-
-    @pl.when(is_dec)
-    def _():
-        prompt_part()
+    for c in stretch_y + kv_copies[2:4]:
+        c.wait_recv()
+    attend(4, 6, 2048, 1536, 0)
+    for c in kv_copies[4:]:
+        c.wait_recv()
 
     def narrow(i, _):
+        attend(8 - 4 * i, 2 + 2 * i, 3584, 1024)
+
         @pl.when(i == 0)
         def _():
-            for c in kv_copies[2:4]:
-                c.wait_recv()
-
-        @pl.when(i == 1)
-        def _():
-            for c in kv_copies[4:]:
-                c.wait_recv()
-
-        attend(
-            jnp.where(i == 1, 8, 4),
-            jnp.where(i == 0, 6, jnp.where(i == 1, 2, 4)),
-            pl.multiple_of(jnp.where(i == 0, 2560, 3584), half),
-            1024,
-        )
-
-        @pl.when(i == 1)
-        def _():
             send_far()
 
         return 0
 
-    lax.fori_loop(0, 3, narrow, 0)
+    lax.fori_loop(0, 2, narrow, 0)
     send_near()
+
+    @pl.when(is_dec)
+    def _():
+        prompt_part()
 
     def rest(i, _):
         @pl.when(is_pre)
@@ -501,7 +493,7 @@
     def _():
         decode_last()
 
-    for c in kv_copies + stretch_y + [far_q_pre] + far_pre + near_pre[0] + near_pre[1]:
+    for c in kv_copies[2:] + stretch_y + [far_q_pre] + far_pre + near_pre[0] + near_pre[1]:
         c.wait_send()
 
     @pl.when(is_pre)

time: 58.4 us -> 53.4 us (0.914)
  Pallas kernels: 54.6 us -> 49.5 us
    pallas_call x1, Pallas kernels: 54.6 us -> 49.5 us  [body(): pl.pallas_call(kernel, out_shape=jax.ShapeDtypeStruct((1024, D), BF16), i...]
where the time goes in v3:
time: 53.4 us; the launch traced here: 53.1 us
  Pallas kernels  49.5 us (93%)
  local copies, waits for them, and re-layouts  3.6 us (7%)
    pallas_call x1, Pallas kernels, body(): pl.pallas_call(kernel, out_shape=jax.ShapeDtypeStruct((1024, D), BF16), i...  49.5 us

profile of v3, /device:TPU:4, one launch (start us, length us, event | category | flops | bytes accessed | tf_op | source)
XLA Modules:
  0.0 53.1 jit_solution(268476095110080541)
XLA Ops:
  0.0 1.0 %copy.10 = bf16[16,8,8,128]{3,2,1,0:T(8,128)(2,1)S(1)} copy(bf16[16,8,8,128]{3,1,2,0:T(8,128)(2,1)} %bitcast.16) | data formatting | bytes 524288
  1.0 0.8 %copy.8 = bf16[32,4,8,128]{3,1,2,0:T(4,128)(2,1)} copy(bf16[32,4,8,128]{3,2,1,0:T(8,128)(2,1)S(1)} %bitcast.15) | data formatting | bytes 524288 | tf_op jit(solution)/shard_map/reshape | solution.py:511
  1.8 49.5 %shard_map.73 = bf16[1024,128]{1,0:T(8,128)(2,1)} custom-call(s32[8]{0:T(128)} %lengths_hbm.1, s32[512]{0:T(512)} %cache_len_hbm.1, s32[8]{0:T(128)} %slots_hbm.1, bf16[1024,128]{1,0:T(8,128)(2,1)} %bitcast.17, bf16[128,256]{1,0:T(8,128)(2,1)} %bitcast.21, bf16[1024,256]{1,0:T(8,128)(2,1)} %bitcast.20, bf16[32,512,256]{2,1,0:T(8,128)(2,1)} %bitcast.19), custom_call_target="tpu_custom_call" | custom-call | flops 10000000000 | bytes 10000000 | tf_op jit(solution)/shard_map/pallas_call | solution.py:518
  51.3 1.0 %copy.9 = bf16[32,4,8,128]{3,2,1,0:T(8,128)(2,1)S(1)} copy(bf16[32,4,8,128]{3,1,2,0:T(4,128)(2,1)} %bitcast.18) | data formatting | bytes 524288 | tf_op jit(solution)/shard_map/transpose | solution.py:561
  52.3 0.8 %reshape.27 = bf16[1,128,1024]{2,1,0:T(8,128)(2,1)} reshape(bf16[32,4,8,128]{3,2,1,0:T(8,128)(2,1)S(1)} %copy.9) | data formatting | bytes 524288 | tf_op jit(solution)/shard_map/reshape | solution.py:561

commit v4 on v3

--- a/solution.py
+++ b/solution.py
@@ -224,7 +224,7 @@
         home_zh = jnp.where(own, zh, jnp.where(near, zh + jnp.where(is_pre, 3, 1), zh + 2))
         home_zh = lax.rem(home_zh, 4)
         index = index - jnp.where(own, 0, jnp.where(near, 1024, jnp.where(is_pre, 2048 - half, 2048)))
-        place = (home_zh * 4 + y) * 128 + (index // 32) * 4 + lax.rem(index, 4)
+        place = (home_zh * 4 + y) * 128 + index // 8
         begin = jnp.zeros_like(place)
         for e in ends[:-1]:
             begin = jnp.where(place >= e, e, begin)
@@ -236,7 +236,7 @@
         rows = block(0, i)
         index = lax.broadcasted_iota(jnp.int32, (RB, D), 0) + i * RB
         key = lax.broadcasted_iota(jnp.int32, (RB, D), 1)
-        mask = (key // 4 == index // 32) & (lax.rem(key, 4) <= lax.rem(index, 4))
+        mask = (key // 4 == index // 32) & (lax.rem(key, 4) <= lax.rem(index // 8, 4))
         small(qall[rows, :], new_ref[...], mask, rows, m, l, acc)
         return 0
 
@@ -508,7 +508,7 @@
 
 
 def body(queries, new_kv, prefix_kv, cache_kv, prompt_lengths, cache_lengths, prompt_slots):
-    q = queries.reshape(32, 4, 8, D).transpose(0, 2, 1, 3).reshape(1024, D)
+    q = queries.reshape(1024, D)
     new = new_kv.reshape(128, 2 * D)
     prefix = prefix_kv.reshape(1024, 2 * D)
     cache = cache_kv.reshape(32, 512, 2 * D)
@@ -558,7 +558,7 @@
         ),
         cost_estimate=pl.CostEstimate(flops=10**10, bytes_accessed=10**7, transcendentals=10**7),
     )(prompt_lengths, cache_lengths, prompt_slots, q, new, prefix, cache)
-    return out.reshape(32, 8, 4, D).transpose(0, 2, 1, 3).reshape(1, 128, 1024)
+    return out.reshape(1, 128, 1024)
 
 
 def solution(mesh):

time: 53.4 us -> 53.1 us (level)
    reshape x2, local copies, waits for them, and re-layouts: 1.62 us -> 3.53 us  [the longest x1 1.77 us: body(): return out.reshape(1, 128, 1024)]
    unnamed x1 -> x0, local copies, waits for them, and re-layouts: 0.99 us -> none
    transpose x1 -> x0, local copies, waits for them, and re-layouts: 0.99 us -> none  [body(): return out.reshape(32, 8, 4, D).transpose(0, 2, 1, 3).reshape(1, 128, 1024)]
where the time goes in v4:
time: 53.1 us; the launch traced here: 52.8 us
  Pallas kernels  49.2 us (93%)
  local copies, waits for them, and re-layouts  3.53 us (7%)
    pallas_call x1, Pallas kernels, body(): pl.pallas_call(kernel, out_shape=jax.ShapeDtypeStruct((1024, D), BF16), i...  49.2 us
    reshape x1, local copies, waits for them, and re-layouts, body(): return out.reshape(1, 128, 1024)  1.77 us
    reshape x1, local copies, waits for them, and re-layouts, body(): q = queries.reshape(1024, D)  1.77 us

profile of v4, /device:TPU:4, one launch (start us, length us, event | category | flops | bytes accessed | tf_op | source)
XLA Modules:
  0.0 52.8 jit_solution(10107987754907603438)
XLA Ops:
  0.0 1.8 %reshape.15.q_ref = bf16[1024,128]{1,0:T(8,128)(2,1)} reshape(bf16[1,128,1024]{2,1,0:T(8,128)(2,1)} %param.7) | data formatting | bytes 524288 | tf_op jit(solution)/shard_map/reshape | solution.py:511
  1.8 49.2 %shard_map.73 = bf16[1024,128]{1,0:T(8,128)(2,1)} custom-call(s32[8]{0:T(128)} %lengths_hbm.1, s32[512]{0:T(512)} %cache_len_hbm.1, s32[8]{0:T(128)} %slots_hbm.1, bf16[1024,128]{1,0:T(8,128)(2,1)} %reshape.15.q_ref, bf16[128,256]{1,0:T(8,128)(2,1)} %bitcast.5, bf16[1024,256]{1,0:T(8,128)(2,1)} %bitcast.4, bf16[32,512,256]{2,1,0:T(8,128)(2,1)} %bitcast.3), custom_call_target="tpu_custom_call" | custom-call | flops 10000000000 | bytes 10000000 | tf_op jit(solution)/shard_map/pallas_call | solution.py:518
  51.0 1.8 %reshape.19 = bf16[1,128,1024]{2,1,0:T(8,128)(2,1)} reshape(bf16[1024,128]{1,0:T(8,128)(2,1)} %shard_map.73) | data formatting | bytes 524288 | tf_op jit(solution)/shard_map/reshape | solution.py:561

commit v5 on v4

--- a/solution.py
+++ b/solution.py
@@ -436,14 +436,14 @@
 
     for c in kv_copies[:2]:
         c.wait_recv()
+    for c in kv_copies[4:]:
+        c.start()
     q_copies[0].wait_recv()
     start_all([far_q_pre], [far_q_dec])
 
     def wide(i, _):
         @pl.when(i == 1)
         def _():
-            for c in kv_copies[4:]:
-                c.start()
             far_q_pre.wait_recv()
 
         attend(4 + 4 * i, 4 - 2 * i, 0, 2048)

time: 53.1 us -> 53.2 us (level)
  the two profiles are of different devices: /device:TPU:4 before, /device:TPU:103 now
where the time goes in v5:
time: 53.2 us; the launch traced here: 53 us
  Pallas kernels  49.5 us (93%)
  local copies, waits for them, and re-layouts  3.53 us (7%)
    pallas_call x1, Pallas kernels, body(): pl.pallas_call(kernel, out_shape=jax.ShapeDtypeStruct((1024, D), BF16), i...  49.5 us
    reshape x1, local copies, waits for them, and re-layouts, body(): return out.reshape(1, 128, 1024)  1.77 us
    reshape x1, local copies, waits for them, and re-layouts, body(): q = queries.reshape(1024, D)  1.77 us

profile of v5, /device:TPU:103, one launch (start us, length us, event | category | flops | bytes accessed | tf_op | source)
XLA Modules:
  0.0 53.0 jit_solution(10890374214948572681)
XLA Ops:
  0.0 1.8 %reshape.15.q_ref = bf16[1024,128]{1,0:T(8,128)(2,1)} reshape(bf16[1,128,1024]{2,1,0:T(8,128)(2,1)} %param.7) | data formatting | bytes 524288 | tf_op jit(solution)/shard_map/reshape | solution.py:511
  1.8 49.5 %shard_map.73 = bf16[1024,128]{1,0:T(8,128)(2,1)} custom-call(s32[8]{0:T(128)} %lengths_hbm.1, s32[512]{0:T(512)} %cache_len_hbm.1, s32[8]{0:T(128)} %slots_hbm.1, bf16[1024,128]{1,0:T(8,128)(2,1)} %reshape.15.q_ref, bf16[128,256]{1,0:T(8,128)(2,1)} %bitcast.5, bf16[1024,256]{1,0:T(8,128)(2,1)} %bitcast.4, bf16[32,512,256]{2,1,0:T(8,128)(2,1)} %bitcast.3), custom_call_target="tpu_custom_call" | custom-call | flops 10000000000 | bytes 10000000 | tf_op jit(solution)/shard_map/pallas_call | solution.py:518
  51.2 1.8 %reshape.19 = bf16[1,128,1024]{2,1,0:T(8,128)(2,1)} reshape(bf16[1024,128]{1,0:T(8,128)(2,1)} %shard_map.73) | data formatting | bytes 524288 | tf_op jit(solution)/shard_map/reshape | solution.py:561
